TPU v7x, 128 devices: a whole 4x4x4 slice. The times are simulated.
128 devices in a mesh: state: 4 (over x), member: 32 (over z, y, core).
Axes of the slice: x: 4, y: 4, z: 4, core: 2. Of those that a mesh axis runs over, the one named last changes fastest.
Arguments:
- ensemble: bfloat16 [256, 131072], P('member', 'state'), may hold values from -8 to 8
- obs_count: int32 [256], replicated, may hold values from 0 to 11
Outputs:
- analysis: bfloat16 [256, 131072], P('member', 'state')
All inputs are finite; a program needn't handle non-finite values.
Results may differ from a plain program's by a relative error of at most 0.0065.
Values may be sent and summed in bfloat16 or wider, within the bound.
A program may use at most 64 MiB of HBM per device.

v0:
```python
import jax
import jax.numpy as jnp
from jax import lax
from jax.sharding import PartitionSpec as P

SWEEPS = 20


def merged(x, axis, combine):
    everything = jax.tree.map(lambda part: lax.all_gather(part, axis), x)
    initial = jax.tree.map(lambda part: part[0], everything)

    def turn(k, so_far):
        return combine(so_far, jax.tree.map(lambda part: part[k], everything))

    return lax.fori_loop(1, lax.axis_size(axis), turn, initial)


def logsum(values, axis):
    top = jnp.max(values, axis=axis, keepdims=True)
    return jnp.squeeze(top, axis) + jnp.log(jnp.sum(jnp.exp(values - top), axis=axis))


def combine(first, second):
    top = jnp.maximum(first[0], second[0])
    return (top, first[1] * jnp.exp(first[0] - top) + second[1] * jnp.exp(second[0] - top))


def per_device(ensemble, obs_count):
    rows = ensemble.shape[0]
    total = ensemble.shape[1] * lax.axis_size("state")
    scale_cost = 16.0 / jnp.float32(total)
    raw_weight = -2.0 * obs_count.astype(jnp.float32)
    logw = raw_weight - jnp.log(jnp.sum(jnp.exp(raw_weight)))
    members = obs_count.shape[0]
    log_count = jnp.log(jnp.float32(members))
    full = lax.all_gather(ensemble, "member", axis=0, tiled=True)
    start = lax.axis_index("member") * rows
    partial_value = lax.dot_general(
        ensemble, full, (((1,), (1,)), ((), ())), preferred_element_type=jnp.float32
    )
    squares = jnp.einsum("ms,ms->m", full, full, preferred_element_type=jnp.float32)
    gram_rows, norms = lax.psum((partial_value, squares), "state")
    own_norms = lax.dynamic_slice_in_dim(norms, start, rows)
    cost_rows = (own_norms[:, None] + norms[None, :] - 2.0 * gram_rows) * scale_cost
    own_logw = lax.dynamic_slice_in_dim(logw, start, rows)

    def sweep_owned(index, carry):
        f_own, g_pot = carry
        f_own = own_logw - logsum(g_pot[None, :] - cost_rows, 1)
        scores = f_own[:, None] - cost_rows
        top = jnp.max(scores, axis=0)
        sums = jnp.sum(jnp.exp(scores - top[None, :]), axis=0)
        top, sums = merged((top, sums), "member", combine)
        g_pot = -log_count - (top + jnp.log(sums))
        return (f_own, g_pot)

    f_own, g_pot = lax.fori_loop(
        0,
        SWEEPS,
        sweep_owned,
        (jnp.zeros((rows,), jnp.float32), jnp.zeros((members,), jnp.float32)),
    )
    plan_part = (members * jnp.exp(f_own[:, None] + g_pot[None, :] - cost_rows)).astype(
        jnp.bfloat16
    )
    plan = lax.all_gather(plan_part, "member", axis=0, tiled=True)
    plan_cols = lax.dynamic_slice_in_dim(plan, start, rows, 1)
    result = lax.dot_general(
        plan_cols, full, (((0,), (0,)), ((), ())), preferred_element_type=jnp.float32
    )
    analysis = result.astype(jnp.bfloat16)
    return analysis


def solution(mesh):
    placed = (P("member", "state"), P())
    return jax.shard_map(
        per_device, mesh=mesh, in_specs=placed, out_specs=P("member", "state"), check_vma=False
    )
```

profile of v0, /device:TPU:1, one launch (start us, length us, event | category | flops | bytes accessed | tf_op | source)
XLA Modules:
  0.0 1110.1 jit_solution(15052123015271228203)
XLA Ops:
  10.2 75.7 %all-gather.12.cloned.1.call-done = bf16[256,32768]{1,0:T(8,128)(2,1)} async-done(((bf16[8,32768]{1,0:T(8,128)(2,1)}), bf16[256,32768]{1,0:T(8,128)(2,1)}) %all-gather.12.cloned.1.call-update) | async-done | bytes 16777232 | tf_op jit(solution)/shard_map/all_gather | solution.py:37
  112.1 957.7 %while.43 = (s32[]{:T(128)}, f32[8]{0:T(128)}, f32[256]{0:T(256)S(1)}, f32[8,256]{1,0:T(8,128)S(1)}, f32[8]{0:T(128)S(1)}, /*index=5*/s32[]{:T(128)}, s32[]{:T(128)}, s32[]{:T(128)}, s32[]{:T(128)}, s32[]{:T(128)}) while((s32[]{:T(128)}, f32[8]{0:T(128)}, f32[256]{0:T(256)S(1)}, f32[8,256]{1,0:T(8,128)S(1)}, f32[8]{0:T(128)S(1)}, ...), condition=%wide.region_10.0_spmd.clone, body=%wide.region_3.0_spmd.clone.sunk | while | flops 22280 | bytes 256750 | solution.py:58
  112.6 25.9 %all-gather.9 = f32[32,1,256]{2,1,0:T(1,128)S(1)} all-gather(f32[1,1,256]{2,1,0:T(1,128)S(1)} %bitcast.38), channel_id=3, replica_groups=mesh['state'=4,'member'=32] {'member'}, dimensions={0}, use_global_device_ids=true | all-gather | bytes 33792 | tf_op jit(solution)/shard_map/while/body/eval_jaxpr/all_gather | solution.py:10
  138.5 21.9 %all-gather.8 = f32[32,1,256]{2,1,0:T(1,128)S(1)} all-gather(f32[1,1,256]{2,1,0:T(1,128)S(1)} %bitcast.37), channel_id=2, replica_groups=mesh['state'=4,'member'=32] {'member'}, dimensions={0}, use_global_device_ids=true | all-gather | bytes 33792 | tf_op jit(solution)/shard_map/while/body/eval_jaxpr/all_gather | solution.py:10
  162.8 23.5 %all-gather.9 = f32[32,1,256]{2,1,0:T(1,128)S(1)} all-gather(f32[1,1,256]{2,1,0:T(1,128)S(1)} %bitcast.38), channel_id=3, replica_groups=mesh['state'=4,'member'=32] {'member'}, dimensions={0}, use_global_device_ids=true | all-gather | bytes 33792 | tf_op jit(solution)/shard_map/while/body/eval_jaxpr/all_gather | solution.py:10
  186.3 21.9 %all-gather.8 = f32[32,1,256]{2,1,0:T(1,128)S(1)} all-gather(f32[1,1,256]{2,1,0:T(1,128)S(1)} %bitcast.37), channel_id=2, replica_groups=mesh['state'=4,'member'=32] {'member'}, dimensions={0}, use_global_device_ids=true | all-gather | bytes 33792 | tf_op jit(solution)/shard_map/while/body/eval_jaxpr/all_gather | solution.py:10
  210.6 23.5 %all-gather.9 = f32[32,1,256]{2,1,0:T(1,128)S(1)} all-gather(f32[1,1,256]{2,1,0:T(1,128)S(1)} %bitcast.38), channel_id=3, replica_groups=mesh['state'=4,'member'=32] {'member'}, dimensions={0}, use_global_device_ids=true | all-gather | bytes 33792 | tf_op jit(solution)/shard_map/while/body/eval_jaxpr/all_gather | solution.py:10
  234.1 21.9 %all-gather.8 = f32[32,1,256]{2,1,0:T(1,128)S(1)} all-gather(f32[1,1,256]{2,1,0:T(1,128)S(1)} %bitcast.37), channel_id=2, replica_groups=mesh['state'=4,'member'=32] {'member'}, dimensions={0}, use_global_device_ids=true | all-gather | bytes 33792 | tf_op jit(solution)/shard_map/while/body/eval_jaxpr/all_gather | solution.py:10
  258.3 23.5 %all-gather.9 = f32[32,1,256]{2,1,0:T(1,128)S(1)} all-gather(f32[1,1,256]{2,1,0:T(1,128)S(1)} %bitcast.38), channel_id=3, replica_groups=mesh['state'=4,'member'=32] {'member'}, dimensions={0}, use_global_device_ids=true | all-gather | bytes 33792 | tf_op jit(solution)/shard_map/while/body/eval_jaxpr/all_gather | solution.py:10
  281.8 21.9 %all-gather.8 = f32[32,1,256]{2,1,0:T(1,128)S(1)} all-gather(f32[1,1,256]{2,1,0:T(1,128)S(1)} %bitcast.37), channel_id=2, replica_groups=mesh['state'=4,'member'=32] {'member'}, dimensions={0}, use_global_device_ids=true | all-gather | bytes 33792 | tf_op jit(solution)/shard_map/while/body/eval_jaxpr/all_gather | solution.py:10
  306.1 23.5 %all-gather.9 = f32[32,1,256]{2,1,0:T(1,128)S(1)} all-gather(f32[1,1,256]{2,1,0:T(1,128)S(1)} %bitcast.38), channel_id=3, replica_groups=mesh['state'=4,'member'=32] {'member'}, dimensions={0}, use_global_device_ids=true | all-gather | bytes 33792 | tf_op jit(solution)/shard_map/while/body/eval_jaxpr/all_gather | solution.py:10
  353.9 23.5 %all-gather.9 = f32[32,1,256]{2,1,0:T(1,128)S(1)} all-gather(f32[1,1,256]{2,1,0:T(1,128)S(1)} %bitcast.38), channel_id=3, replica_groups=mesh['state'=4,'member'=32] {'member'}, dimensions={0}, use_global_device_ids=true | all-gather | bytes 33792 | tf_op jit(solution)/shard_map/while/body/eval_jaxpr/all_gather | solution.py:10
  401.6 23.5 %all-gather.9 = f32[32,1,256]{2,1,0:T(1,128)S(1)} all-gather(f32[1,1,256]{2,1,0:T(1,128)S(1)} %bitcast.38), channel_id=3, replica_groups=mesh['state'=4,'member'=32] {'member'}, dimensions={0}, use_global_device_ids=true | all-gather | bytes 33792 | tf_op jit(solution)/shard_map/while/body/eval_jaxpr/all_gather | solution.py:10
  449.4 23.5 %all-gather.9 = f32[32,1,256]{2,1,0:T(1,128)S(1)} all-gather(f32[1,1,256]{2,1,0:T(1,128)S(1)} %bitcast.38), channel_id=3, replica_groups=mesh['state'=4,'member'=32] {'member'}, dimensions={0}, use_global_device_ids=true | all-gather | bytes 33792 | tf_op jit(solution)/shard_map/while/body/eval_jaxpr/all_gather | solution.py:10
  497.1 23.5 %all-gather.9 = f32[32,1,256]{2,1,0:T(1,128)S(1)} all-gather(f32[1,1,256]{2,1,0:T(1,128)S(1)} %bitcast.38), channel_id=3, replica_groups=mesh['state'=4,'member'=32] {'member'}, dimensions={0}, use_global_device_ids=true | all-gather | bytes 33792 | tf_op jit(solution)/shard_map/while/body/eval_jaxpr/all_gather | solution.py:10
  544.9 23.5 %all-gather.9 = f32[32,1,256]{2,1,0:T(1,128)S(1)} all-gather(f32[1,1,256]{2,1,0:T(1,128)S(1)} %bitcast.38), channel_id=3, replica_groups=mesh['state'=4,'member'=32] {'member'}, dimensions={0}, use_global_device_ids=true | all-gather | bytes 33792 | tf_op jit(solution)/shard_map/while/body/eval_jaxpr/all_gather | solution.py:10
  592.7 23.5 %all-gather.9 = f32[32,1,256]{2,1,0:T(1,128)S(1)} all-gather(f32[1,1,256]{2,1,0:T(1,128)S(1)} %bitcast.38), channel_id=3, replica_groups=mesh['state'=4,'member'=32] {'member'}, dimensions={0}, use_global_device_ids=true | all-gather | bytes 33792 | tf_op jit(solution)/shard_map/while/body/eval_jaxpr/all_gather | solution.py:10
  640.4 23.5 %all-gather.9 = f32[32,1,256]{2,1,0:T(1,128)S(1)} all-gather(f32[1,1,256]{2,1,0:T(1,128)S(1)} %bitcast.38), channel_id=3, replica_groups=mesh['state'=4,'member'=32] {'member'}, dimensions={0}, use_global_device_ids=true | all-gather | bytes 33792 | tf_op jit(solution)/shard_map/while/body/eval_jaxpr/all_gather | solution.py:10
  688.2 23.5 %all-gather.9 = f32[32,1,256]{2,1,0:T(1,128)S(1)} all-gather(f32[1,1,256]{2,1,0:T(1,128)S(1)} %bitcast.38), channel_id=3, replica_groups=mesh['state'=4,'member'=32] {'member'}, dimensions={0}, use_global_device_ids=true | all-gather | bytes 33792 | tf_op jit(solution)/shard_map/while/body/eval_jaxpr/all_gather | solution.py:10
  735.9 23.5 %all-gather.9 = f32[32,1,256]{2,1,0:T(1,128)S(1)} all-gather(f32[1,1,256]{2,1,0:T(1,128)S(1)} %bitcast.38), channel_id=3, replica_groups=mesh['state'=4,'member'=32] {'member'}, dimensions={0}, use_global_device_ids=true | all-gather | bytes 33792 | tf_op jit(solution)/shard_map/while/body/eval_jaxpr/all_gather | solution.py:10
  783.7 23.5 %all-gather.9 = f32[32,1,256]{2,1,0:T(1,128)S(1)} all-gather(f32[1,1,256]{2,1,0:T(1,128)S(1)} %bitcast.38), channel_id=3, replica_groups=mesh['state'=4,'member'=32] {'member'}, dimensions={0}, use_global_device_ids=true | all-gather | bytes 33792 | tf_op jit(solution)/shard_map/while/body/eval_jaxpr/all_gather | solution.py:10
  807.2 21.9 %all-gather.8 = f32[32,1,256]{2,1,0:T(1,128)S(1)} all-gather(f32[1,1,256]{2,1,0:T(1,128)S(1)} %bitcast.37), channel_id=2, replica_groups=mesh['state'=4,'member'=32] {'member'}, dimensions={0}, use_global_device_ids=true | all-gather | bytes 33792 | tf_op jit(solution)/shard_map/while/body/eval_jaxpr/all_gather | solution.py:10
  831.5 23.5 %all-gather.9 = f32[32,1,256]{2,1,0:T(1,128)S(1)} all-gather(f32[1,1,256]{2,1,0:T(1,128)S(1)} %bitcast.38), channel_id=3, replica_groups=mesh['state'=4,'member'=32] {'member'}, dimensions={0}, use_global_device_ids=true | all-gather | bytes 33792 | tf_op jit(solution)/shard_map/while/body/eval_jaxpr/all_gather | solution.py:10
  855.0 21.9 %all-gather.8 = f32[32,1,256]{2,1,0:T(1,128)S(1)} all-gather(f32[1,1,256]{2,1,0:T(1,128)S(1)} %bitcast.37), channel_id=2, replica_groups=mesh['state'=4,'member'=32] {'member'}, dimensions={0}, use_global_device_ids=true | all-gather | bytes 33792 | tf_op jit(solution)/shard_map/while/body/eval_jaxpr/all_gather | solution.py:10
  879.2 23.5 %all-gather.9 = f32[32,1,256]{2,1,0:T(1,128)S(1)} all-gather(f32[1,1,256]{2,1,0:T(1,128)S(1)} %bitcast.38), channel_id=3, replica_groups=mesh['state'=4,'member'=32] {'member'}, dimensions={0}, use_global_device_ids=true | all-gather | bytes 33792 | tf_op jit(solution)/shard_map/while/body/eval_jaxpr/all_gather | solution.py:10
  902.7 21.9 %all-gather.8 = f32[32,1,256]{2,1,0:T(1,128)S(1)} all-gather(f32[1,1,256]{2,1,0:T(1,128)S(1)} %bitcast.37), channel_id=2, replica_groups=mesh['state'=4,'member'=32] {'member'}, dimensions={0}, use_global_device_ids=true | all-gather | bytes 33792 | tf_op jit(solution)/shard_map/while/body/eval_jaxpr/all_gather | solution.py:10
  927.0 23.5 %all-gather.9 = f32[32,1,256]{2,1,0:T(1,128)S(1)} all-gather(f32[1,1,256]{2,1,0:T(1,128)S(1)} %bitcast.38), channel_id=3, replica_groups=mesh['state'=4,'member'=32] {'member'}, dimensions={0}, use_global_device_ids=true | all-gather | bytes 33792 | tf_op jit(solution)/shard_map/while/body/eval_jaxpr/all_gather | solution.py:10
  950.5 21.9 %all-gather.8 = f32[32,1,256]{2,1,0:T(1,128)S(1)} all-gather(f32[1,1,256]{2,1,0:T(1,128)S(1)} %bitcast.37), channel_id=2, replica_groups=mesh['state'=4,'member'=32] {'member'}, dimensions={0}, use_global_device_ids=true | all-gather | bytes 33792 | tf_op jit(solution)/shard_map/while/body/eval_jaxpr/all_gather | solution.py:10
  974.8 23.5 %all-gather.9 = f32[32,1,256]{2,1,0:T(1,128)S(1)} all-gather(f32[1,1,256]{2,1,0:T(1,128)S(1)} %bitcast.38), channel_id=3, replica_groups=mesh['state'=4,'member'=32] {'member'}, dimensions={0}, use_global_device_ids=true | all-gather | bytes 33792 | tf_op jit(solution)/shard_map/while/body/eval_jaxpr/all_gather | solution.py:10
  998.3 21.9 %all-gather.8 = f32[32,1,256]{2,1,0:T(1,128)S(1)} all-gather(f32[1,1,256]{2,1,0:T(1,128)S(1)} %bitcast.37), channel_id=2, replica_groups=mesh['state'=4,'member'=32] {'member'}, dimensions={0}, use_global_device_ids=true | all-gather | bytes 33792 | tf_op jit(solution)/shard_map/while/body/eval_jaxpr/all_gather | solution.py:10
  1022.5 23.5 %all-gather.9 = f32[32,1,256]{2,1,0:T(1,128)S(1)} all-gather(f32[1,1,256]{2,1,0:T(1,128)S(1)} %bitcast.38), channel_id=3, replica_groups=mesh['state'=4,'member'=32] {'member'}, dimensions={0}, use_global_device_ids=true | all-gather | bytes 33792 | tf_op jit(solution)/shard_map/while/body/eval_jaxpr/all_gather | solution.py:10
  1070.4 23.9 %all_gather.31 = bf16[256,256]{1,0:T(8,128)(2,1)S(1)} all-gather(bf16[8,256]{1,0:T(8,128)(2,1)S(1)} %multiply_convert_fusion), channel_id=1, replica_groups=mesh['state'=4,'member'=32] {'member'}, dimensions={0}, use_global_device_ids=true | all-gather | bytes 135168 | tf_op jit(solution)/shard_map/all_gather | solution.py:67
  (1547 shorter events, 345.1 us)
Async XLA Ops:
  6.5 86.6 %copy-start = (bf16[8,32768]{1,0:T(8,128)(2,1)S(1)}, bf16[8,32768]{1,0:T(8,128)(2,1)}, u32[]{:S(2)}) copy-start(bf16[8,32768]{1,0:T(8,128)(2,1)} %param.6) | copy-start | bytes 1572868
  6.5 79.4 %all-gather.12.cloned.1.call-start = ((), (), s32[]{:S(2)}) async-start(), calls=%async_computation | async-start | bytes 17301504 | tf_op jit(solution)/shard_map/all_gather | solution.py:37
  112.4 49.9 %copy-start.1 = (f32[8]{0:T(128)}, f32[8]{0:T(128)S(1)}, u32[]{:S(2)}) copy-start(f32[8]{0:T(128)S(1)} %add_subtract_fusion.4) | copy-start | bytes 100 | tf_op jit(solution)/shard_map/while
  162.6 47.4 %copy-start.1 = (f32[8]{0:T(128)}, f32[8]{0:T(128)S(1)}, u32[]{:S(2)}) copy-start(f32[8]{0:T(128)S(1)} %add_subtract_fusion.4) | copy-start | bytes 100 | tf_op jit(solution)/shard_map/while
  210.4 47.4 %copy-start.1 = (f32[8]{0:T(128)}, f32[8]{0:T(128)S(1)}, u32[]{:S(2)}) copy-start(f32[8]{0:T(128)S(1)} %add_subtract_fusion.4) | copy-start | bytes 100 | tf_op jit(solution)/shard_map/while
  258.1 47.4 %copy-start.1 = (f32[8]{0:T(128)}, f32[8]{0:T(128)S(1)}, u32[]{:S(2)}) copy-start(f32[8]{0:T(128)S(1)} %add_subtract_fusion.4) | copy-start | bytes 100 | tf_op jit(solution)/shard_map/while
  305.9 47.4 %copy-start.1 = (f32[8]{0:T(128)}, f32[8]{0:T(128)S(1)}, u32[]{:S(2)}) copy-start(f32[8]{0:T(128)S(1)} %add_subtract_fusion.4) | copy-start | bytes 100 | tf_op jit(solution)/shard_map/while
  353.7 47.4 %copy-start.1 = (f32[8]{0:T(128)}, f32[8]{0:T(128)S(1)}, u32[]{:S(2)}) copy-start(f32[8]{0:T(128)S(1)} %add_subtract_fusion.4) | copy-start | bytes 100 | tf_op jit(solution)/shard_map/while
  401.4 47.4 %copy-start.1 = (f32[8]{0:T(128)}, f32[8]{0:T(128)S(1)}, u32[]{:S(2)}) copy-start(f32[8]{0:T(128)S(1)} %add_subtract_fusion.4) | copy-start | bytes 100 | tf_op jit(solution)/shard_map/while
  449.2 47.4 %copy-start.1 = (f32[8]{0:T(128)}, f32[8]{0:T(128)S(1)}, u32[]{:S(2)}) copy-start(f32[8]{0:T(128)S(1)} %add_subtract_fusion.4) | copy-start | bytes 100 | tf_op jit(solution)/shard_map/while
  496.9 47.4 %copy-start.1 = (f32[8]{0:T(128)}, f32[8]{0:T(128)S(1)}, u32[]{:S(2)}) copy-start(f32[8]{0:T(128)S(1)} %add_subtract_fusion.4) | copy-start | bytes 100 | tf_op jit(solution)/shard_map/while
  544.7 47.4 %copy-start.1 = (f32[8]{0:T(128)}, f32[8]{0:T(128)S(1)}, u32[]{:S(2)}) copy-start(f32[8]{0:T(128)S(1)} %add_subtract_fusion.4) | copy-start | bytes 100 | tf_op jit(solution)/shard_map/while
  592.5 47.4 %copy-start.1 = (f32[8]{0:T(128)}, f32[8]{0:T(128)S(1)}, u32[]{:S(2)}) copy-start(f32[8]{0:T(128)S(1)} %add_subtract_fusion.4) | copy-start | bytes 100 | tf_op jit(solution)/shard_map/while
  640.2 47.4 %copy-start.1 = (f32[8]{0:T(128)}, f32[8]{0:T(128)S(1)}, u32[]{:S(2)}) copy-start(f32[8]{0:T(128)S(1)} %add_subtract_fusion.4) | copy-start | bytes 100 | tf_op jit(solution)/shard_map/while
  688.0 47.4 %copy-start.1 = (f32[8]{0:T(128)}, f32[8]{0:T(128)S(1)}, u32[]{:S(2)}) copy-start(f32[8]{0:T(128)S(1)} %add_subtract_fusion.4) | copy-start | bytes 100 | tf_op jit(solution)/shard_map/while
  735.8 47.4 %copy-start.1 = (f32[8]{0:T(128)}, f32[8]{0:T(128)S(1)}, u32[]{:S(2)}) copy-start(f32[8]{0:T(128)S(1)} %add_subtract_fusion.4) | copy-start | bytes 100 | tf_op jit(solution)/shard_map/while
  783.5 47.4 %copy-start.1 = (f32[8]{0:T(128)}, f32[8]{0:T(128)S(1)}, u32[]{:S(2)}) copy-start(f32[8]{0:T(128)S(1)} %add_subtract_fusion.4) | copy-start | bytes 100 | tf_op jit(solution)/shard_map/while
  831.3 47.4 %copy-start.1 = (f32[8]{0:T(128)}, f32[8]{0:T(128)S(1)}, u32[]{:S(2)}) copy-start(f32[8]{0:T(128)S(1)} %add_subtract_fusion.4) | copy-start | bytes 100 | tf_op jit(solution)/shard_map/while
  879.0 47.4 %copy-start.1 = (f32[8]{0:T(128)}, f32[8]{0:T(128)S(1)}, u32[]{:S(2)}) copy-start(f32[8]{0:T(128)S(1)} %add_subtract_fusion.4) | copy-start | bytes 100 | tf_op jit(solution)/shard_map/while
  926.8 47.4 %copy-start.1 = (f32[8]{0:T(128)}, f32[8]{0:T(128)S(1)}, u32[]{:S(2)}) copy-start(f32[8]{0:T(128)S(1)} %add_subtract_fusion.4) | copy-start | bytes 100 | tf_op jit(solution)/shard_map/while
  974.6 47.4 %copy-start.1 = (f32[8]{0:T(128)}, f32[8]{0:T(128)S(1)}, u32[]{:S(2)}) copy-start(f32[8]{0:T(128)S(1)} %add_subtract_fusion.4) | copy-start | bytes 100 | tf_op jit(solution)/shard_map/while
  1022.3 47.4 %copy-start.1 = (f32[8]{0:T(128)}, f32[8]{0:T(128)S(1)}, u32[]{:S(2)}) copy-start(f32[8]{0:T(128)S(1)} %add_subtract_fusion.4) | copy-start | bytes 100 | tf_op jit(solution)/shard_map/while
Sparse Core Ops, SparseCore 0:
  9.6 76.2 all-gather.11
where the time goes:
time: 1110 us
  blocking collectives  943 us (85%)
  waiting for transfers between devices  76.5 us (7%)
  other arithmetic  32.8 us (3%)
  matrix products  19.1 us (2%)
  loops' own time  17.3 us (2%)
  between operations  14.2 us (1%)
    all_gather x40, blocking collectives, merged(): everything = jax.tree.map(lambda part: lax.all_gather(part, axis), x)  910 us
    all_gather x1, waiting for transfers between devices, per_device(): full = lax.all_gather(ensemble, 'member', axis=0, tiled=True)  75.7 us
    all_gather x1, blocking collectives, per_device(): plan = lax.all_gather(plan_part, 'member', axis=0, tiled=True)  23.9 us
  transfers between devices with their start and end apart: 1, of which 1 were waited for; matrix products, arithmetic and copies ran while one was open for 0% of the time, Pallas kernels for 0%

commit v1 on v0

v1 whole, which is shorter than its diff:
```python
import functools
import math

import jax
import jax.numpy as jnp
from jax import lax
from jax.experimental import pallas as pl
from jax.experimental.pallas import tpu as pltpu
from jax.sharding import PartitionSpec as P

SWEEPS = 20
MESH = pl.DeviceIdType.MESH
LOG2E = math.log2(math.e)


def member_peer(step, size):
    return lax.rem(lax.axis_index("member") + step, size)


def kernel(
    n_member, n_state, total,
    ens_ref, obs_ref, out_ref,
    slab, part, part_in, rows_in, gram, cost_ref, result,
    own_sem, send_sems, recv_sems,
):
    rows = ens_ref.shape[0]
    cols = ens_ref.shape[1] // n_member
    members = rows * n_member
    me = lax.axis_index("member")
    plane = lax.axis_index("state")

    barrier = pltpu.get_barrier_semaphore()

    def greet(step, carry):
        pl.semaphore_signal(
            barrier, inc=1, device_id={"member": member_peer(step, n_member)}, device_id_type=MESH
        )
        return carry

    lax.fori_loop(1, n_member, greet, 0)
    for step in range(1, n_state):
        pl.semaphore_signal(
            barrier, inc=1, device_id={"state": lax.rem(plane + step, n_state)}, device_id_type=MESH
        )
    pl.semaphore_wait(barrier, n_member - 1 + n_state - 1)

    def to_members(source, target, phase):
        def send(step, carry):
            peer = member_peer(step, n_member)
            pltpu.make_async_remote_copy(
                src_ref=source(peer),
                dst_ref=target,
                send_sem=send_sems.at[phase],
                recv_sem=recv_sems.at[phase],
                device_id={"member": peer},
                device_id_type=MESH,
            ).start()
            return carry

        lax.fori_loop(1, n_member, send, 0)

    def wait_for(ref, sem):
        pltpu.make_async_copy(ref, ref, sem).wait()

    own = pltpu.make_async_copy(
        ens_ref.at[:, pl.ds(pl.multiple_of(me * cols, cols), cols)], slab.at[me], own_sem
    )
    own.start()
    to_members(
        lambda peer: ens_ref.at[:, pl.ds(pl.multiple_of(peer * cols, cols), cols)], slab.at[me], 0
    )

    raw = -2.0 * obs_ref[...].astype(jnp.float32)
    logw_row = (raw - jnp.log(jnp.sum(jnp.exp(raw), axis=1, keepdims=True))) * LOG2E
    eye = lax.broadcasted_iota(jnp.int32, (members, members), 0) == lax.broadcasted_iota(
        jnp.int32, (members, members), 1
    )
    logw = jnp.sum(jnp.where(eye, logw_row, 0.0), axis=1, keepdims=True)

    own.wait()
    wait_for(slab.at[pl.ds(0, n_member - 1)], recv_sems.at[0])

    held = slab[...].reshape(members, cols)
    partial_gram = lax.dot_general(
        held, held, (((1,), (1,)), ((), ())), preferred_element_type=jnp.float32
    )
    part[...] = partial_gram.reshape(n_member, rows, members)

    part_in[me] = part[me]
    to_members(lambda peer: part.at[peer], part_in.at[me], 1)
    wait_for(part.at[pl.ds(0, n_member - 1)], recv_sems.at[1])
    rows_in[plane] = jnp.sum(part_in[...], axis=0)
    for step in range(1, n_state):
        pltpu.make_async_remote_copy(
            src_ref=rows_in.at[plane],
            dst_ref=rows_in.at[plane],
            send_sem=send_sems.at[2],
            recv_sem=recv_sems.at[2],
            device_id={"state": lax.rem(plane + step, n_state)},
            device_id_type=MESH,
        ).start()
    wait_for(rows_in.at[pl.ds(0, n_state - 1)], recv_sems.at[2])
    gram[me] = jnp.sum(rows_in[...], axis=0)
    to_members(lambda peer: gram.at[me], gram.at[me], 3)
    wait_for(gram.at[pl.ds(0, n_member - 1)], recv_sems.at[3])

    whole = gram[...].reshape(members, members)
    diagonal = jnp.where(eye, whole, 0.0)
    norm_col = jnp.sum(diagonal, axis=1, keepdims=True)
    norm_row = jnp.sum(diagonal, axis=0, keepdims=True)
    cost = (norm_col + norm_row - 2.0 * whole) * (16.0 / total * LOG2E)
    cost_ref[...] = cost
    log_count = math.log2(members)

    def sweep(index, carry):
        f_pot, g_pot = carry
        cost = cost_ref[...]
        sums = jnp.sum(jnp.exp2(f_pot + g_pot - cost), axis=1, keepdims=True)
        f_pot = f_pot + logw - jnp.log2(sums)
        sums = jnp.sum(jnp.exp2(f_pot + g_pot - cost), axis=0, keepdims=True)
        g_pot = g_pot - log_count - jnp.log2(sums)
        return (f_pot, g_pot)

    f_pot, g_pot = lax.fori_loop(
        0,
        SWEEPS,
        sweep,
        (jnp.zeros((members, 1), jnp.float32), jnp.zeros((1, members), jnp.float32)),
    )
    cost = cost_ref[...]
    plan = jnp.exp2(f_pot + g_pot - cost + log_count).astype(jnp.bfloat16)
    analysis = lax.dot_general(
        plan, slab[...].reshape(members, cols), (((0,), (0,)), ((), ())),
        preferred_element_type=jnp.float32,
    )
    result[...] = analysis.reshape(n_member, rows, cols).astype(jnp.bfloat16)

    mine = out_ref.at[:, pl.ds(pl.multiple_of(me * cols, cols), cols)]
    own = pltpu.make_async_copy(result.at[me], mine, own_sem)
    own.start()
    to_members(lambda peer: result.at[peer], mine, 4)
    own.wait()
    wait_for(out_ref.at[:, pl.ds(0, (n_member - 1) * cols)], recv_sems.at[4])

    wait_for(slab.at[pl.ds(0, n_member - 1)], send_sems.at[0])
    wait_for(part.at[pl.ds(0, n_member - 1)], send_sems.at[1])
    wait_for(rows_in.at[pl.ds(0, n_state - 1)], send_sems.at[2])
    wait_for(gram.at[pl.ds(0, n_member - 1)], send_sems.at[3])
    wait_for(result.at[pl.ds(0, n_member - 1)], send_sems.at[4])


def per_device(n_member, n_state, ensemble, obs_count):
    rows, width = ensemble.shape
    members, cols = rows * n_member, width // n_member
    return pl.pallas_call(
        functools.partial(kernel, n_member, n_state, width * n_state),
        out_shape=jax.ShapeDtypeStruct((rows, width), jnp.bfloat16),
        in_specs=[pl.BlockSpec(memory_space=pl.ANY), pl.BlockSpec(memory_space=pltpu.VMEM)],
        out_specs=pl.BlockSpec(memory_space=pl.ANY),
        scratch_shapes=[
            pltpu.VMEM((n_member, rows, cols), jnp.bfloat16),
            pltpu.VMEM((n_member, rows, members), jnp.float32),
            pltpu.VMEM((n_member, rows, members), jnp.float32),
            pltpu.VMEM((n_state, rows, members), jnp.float32),
            pltpu.VMEM((n_member, rows, members), jnp.float32),
            pltpu.VMEM((members, members), jnp.float32),
            pltpu.VMEM((n_member, rows, cols), jnp.bfloat16),
            pltpu.SemaphoreType.DMA,
            pltpu.SemaphoreType.DMA((5,)),
            pltpu.SemaphoreType.DMA((5,)),
        ],
        compiler_params=pltpu.CompilerParams(
            collective_id=0, has_side_effects=True, vmem_limit_bytes=32 * 1024 * 1024
        ),
    )(ensemble, obs_count.reshape(1, members))


def solution(mesh):
    body = functools.partial(per_device, mesh.shape["member"], mesh.shape["state"])
    return jax.shard_map(
        body, mesh=mesh, in_specs=(P("member", "state"), P()), out_specs=P("member", "state"),
        check_vma=False,
    )
```

time: 1110 us -> 48.7 us (0.04)
  blocking collectives: 943 us -> 0 us
  waiting for transfers between devices: 76.5 us -> 0 us
  Pallas kernels: 0 us -> 46 us
  other arithmetic: 32.8 us -> 0 us
  matrix products: 19.1 us -> 0 us
  loops' own time: 17.3 us -> 0 us
  between operations: 14.2 us -> 0.01 us
    all_gather x41 -> x0, blocking collectives: 934 us -> none  [the longest x40 910 us: merged(): everything = jax.tree.map(lambda part: lax.all_gather(part, axis), x)]
    all_gather x1 -> x0, waiting for transfers between devices: 75.7 us -> none  [per_device(): full = lax.all_gather(ensemble, 'member', axis=0, tiled=True)]
    pallas_call x0 -> x1, Pallas kernels: none -> 46 us  [per_device(): pl.pallas_call(functools.partial(kernel, n_member, n_state, width * n_sta...]
    dot_general x2 -> x0, matrix products: 19.1 us -> none  [the longest x1 10.2 us: per_device(): lax.dot_general(ensemble, full, (((1,), (1,)), ((), ())), preferred_eleme...]
    another operation x21 -> x0, loops' own time: 17.3 us -> none  [the longest x20 16 us: merged(): return lax.fori_loop(1, lax.axis_size(axis), turn, initial)]
    add x620 -> x0, other arithmetic: 12.7 us -> none  [combine(): first[1] * jnp.exp(first[0] - top) + second[1] * jnp.exp(second[0] - top)]
  transfers between devices with their start and end apart: 1 -> 0, of which waited for: 1 -> 0; matrix products, arithmetic and copies ran while one was open for 0% -> 0% of each run, Pallas kernels for 0% -> 0%
where the time goes in v1:
time: 48.7 us; the launch traced here: 48.5 us
  Pallas kernels  46 us (94%)
  local copies, waits for them, and re-layouts  2.52 us (5%)
    pallas_call x1, Pallas kernels, per_device(): pl.pallas_call(functools.partial(kernel, n_member, n_state, width * n_sta...  46 us
    unnamed x5, local copies, waits for them, and re-layouts  2.52 us

profile of v1, /device:TPU:1, one launch (start us, length us, event | category | flops | bytes accessed | tf_op | source)
XLA Modules:
  0.0 48.5 jit_solution(8758882187716632038)
XLA Ops:
  0.0 0.0 copy-start.1
  0.0 0.7 %copy-done.1 = s32[256]{0:T(256)S(1)} copy-done((s32[256]{0:T(256)S(1)}, s32[256]{0:T(256)}, u32[]{:S(2)}) %copy-start.1) | copy-done | bytes 1048
  0.7 0.0 copy-start
  0.7 1.0 %copy-done = bf16[8,32768]{1,0:T(8,128)(2,1)S(1)} copy-done((bf16[8,32768]{1,0:T(8,128)(2,1)S(1)}, bf16[8,32768]{1,0:T(8,128)(2,1)}, u32[]{:S(2)}) %copy-start) | copy-done | bytes 524312
  1.7 46.0 %shard_map.28 = bf16[8,32768]{1,0:T(8,128)(2,1)S(1)} custom-call(bf16[8,32768]{1,0:T(8,128)(2,1)S(1)} %copy-done, s32[1,256]{1,0:T(1,128)S(1)} %bitcast.1), custom_call_target="tpu_custom_call" | custom-call | tf_op jit(solution)/shard_map/pallas_call | solution.py:155
  47.7 0.8 %copy.4 = bf16[8,32768]{1,0:T(8,128)(2,1)} copy(bf16[8,32768]{1,0:T(8,128)(2,1)S(1)} %shard_map.28) | data formatting | bytes 1048576
Async XLA Ops:
  0.0 0.7 %copy-start.1 = (s32[256]{0:T(256)S(1)}, s32[256]{0:T(256)}, u32[]{:S(2)}) copy-start(s32[256]{0:T(256)} %param.3) | copy-start | bytes 3076
  0.7 1.0 %copy-start = (bf16[8,32768]{1,0:T(8,128)(2,1)S(1)}, bf16[8,32768]{1,0:T(8,128)(2,1)}, u32[]{:S(2)}) copy-start(bf16[8,32768]{1,0:T(8,128)(2,1)} %ens_ref.1) | copy-start | bytes 1572868

commit v2 on v1

v2 whole, which is shorter than its diff:
```python
import functools
import math

import jax
import jax.numpy as jnp
from jax import lax
from jax.experimental import pallas as pl
from jax.experimental.pallas import tpu as pltpu
from jax.sharding import PartitionSpec as P

SWEEPS = 20
MESH = pl.DeviceIdType.MESH
LOG2E = math.log2(math.e)


def hops(offset):
    return sum(min(step, 4 - step) for step in offset[:2])


OFFSETS = sorted(
    ((z, y, c) for z in range(4) for y in range(4) for c in range(2) if (z, y, c) != (0, 0, 0)),
    key=lambda offset: -hops(offset),
)


def member_peers():
    me = lax.axis_index("member")
    z, y, c = lax.div(me, 8), lax.rem(lax.div(me, 2), 4), lax.rem(me, 2)
    return [
        lax.rem(z + dz, 4) * 8 + lax.rem(y + dy, 4) * 2 + lax.rem(c + dc, 2)
        for dz, dy, dc in OFFSETS
    ]


def kernel(
    n_member, n_state, total,
    ens_ref, obs_ref, out_ref,
    slab, obs, part, part_in, rows_in, dist, cost_ref, result,
    own_sems, send_sems, recv_sems,
):
    rows = ens_ref.shape[0]
    cols = ens_ref.shape[1] // n_member
    members = rows * n_member
    half = members // 2
    me = lax.axis_index("member")
    plane = lax.axis_index("state")
    peers = member_peers()
    planes = [lax.rem(plane + step, n_state) for step in range(1, n_state)]

    barrier = pltpu.get_barrier_semaphore()
    for peer in peers:
        pl.semaphore_signal(barrier, inc=1, device_id={"member": peer}, device_id_type=MESH)
    for other in planes:
        pl.semaphore_signal(barrier, inc=1, device_id={"state": other}, device_id_type=MESH)

    def column_block(ref, index):
        return ref.at[:, pl.ds(pl.multiple_of(index * cols, cols), cols)]

    own_obs = pltpu.make_async_copy(obs_ref, obs, own_sems.at[0])
    own_obs.start()
    own_block = pltpu.make_async_copy(column_block(ens_ref, me), slab.at[me], own_sems.at[1])
    own_block.start()
    pl.semaphore_wait(barrier, n_member - 1 + n_state - 1)

    def send(source, target, phase, device):
        pltpu.make_async_remote_copy(
            src_ref=source,
            dst_ref=target,
            send_sem=send_sems.at[phase],
            recv_sem=recv_sems.at[phase],
            device_id=device,
            device_id_type=MESH,
        ).start()

    def wait_for(ref, sem):
        pltpu.make_async_copy(ref, ref, sem).wait()

    for peer in peers:
        send(column_block(ens_ref, peer), slab.at[me], 0, {"member": peer})

    own_obs.wait()
    raw = -2.0 * obs[...].astype(jnp.float32)
    logw = (raw - jnp.log(jnp.sum(jnp.exp(raw), axis=1, keepdims=True))) * LOG2E
    row = lax.broadcasted_iota(jnp.int32, (members, members), 0)
    column = lax.broadcasted_iota(jnp.int32, (members, members), 1)
    eye = row == column
    above = row[:half, :half] < column[:half, :half]

    own_block.wait()
    wait_for(slab.at[pl.ds(0, n_member - 1)], recv_sems.at[0])

    held = slab[...].reshape(members, cols)
    gram = lax.dot_general(
        held, held, (((1,), (1,)), ((), ())), preferred_element_type=jnp.float32
    )
    diagonal = jnp.where(eye, gram, 0.0)
    norm_col = jnp.sum(diagonal, axis=1, keepdims=True)
    norm_row = jnp.sum(diagonal, axis=0, keepdims=True)
    apart = norm_col + norm_row - 2.0 * gram
    folded = jnp.where(above, apart[:half, :half], apart[half:, half:])
    part[: n_member // 2] = folded.reshape(n_member // 2, rows, half)
    part[n_member // 2 :] = apart[:half, half:].reshape(n_member // 2, rows, half)

    for peer in peers:
        send(part.at[peer], part_in.at[me], 1, {"member": peer})
    part_in[me] = part[me]
    wait_for(part.at[pl.ds(0, n_member - 1)], recv_sems.at[1])
    rows_in[plane] = jnp.sum(part_in[...], axis=0)
    for other in planes:
        send(rows_in.at[plane], rows_in.at[plane], 2, {"state": other})
    wait_for(rows_in.at[pl.ds(0, n_state - 1)], recv_sems.at[2])
    dist[me] = jnp.sum(rows_in[...], axis=0)
    for peer in peers:
        send(dist.at[me], dist.at[me], 3, {"member": peer})
    wait_for(dist.at[pl.ds(0, n_member - 1)], recv_sems.at[3])

    scale_cost = 16.0 / total * LOG2E
    folded = dist[: n_member // 2].reshape(half, half) * scale_cost
    across = dist[n_member // 2 :].reshape(half, half) * scale_cost
    first = jnp.where(above, folded, 0.0)
    second = folded - first
    cost_ref[:half, :half] = first + first.T
    cost_ref[half:, half:] = second + second.T
    cost_ref[:half, half:] = across
    cost_ref[half:, :half] = across.T
    log_count = math.log2(members)

    def sweep(index, carry):
        f_pot, g_pot = carry
        cost = cost_ref[...]
        sums = jnp.sum(jnp.exp2(g_pot + f_pot - cost), axis=0, keepdims=True)
        f_pot = f_pot + logw - jnp.log2(sums)
        sums = jnp.sum(jnp.exp2(g_pot + f_pot - cost), axis=1, keepdims=True)
        g_pot = g_pot - log_count - jnp.log2(sums)
        return (f_pot, g_pot)

    f_pot, g_pot = lax.fori_loop(
        0,
        SWEEPS,
        sweep,
        (jnp.zeros((1, members), jnp.float32), jnp.zeros((members, 1), jnp.float32)),
    )
    plan = jnp.exp2(g_pot + f_pot - cost_ref[...] + log_count).astype(jnp.bfloat16)
    analysis = lax.dot_general(
        plan, slab[...].reshape(members, cols), (((1,), (0,)), ((), ())),
        preferred_element_type=jnp.float32,
    )
    result[...] = analysis.reshape(n_member, rows, cols).astype(jnp.bfloat16)

    mine = column_block(out_ref, me)
    for peer in peers:
        send(result.at[peer], mine, 4, {"member": peer})
    own_block = pltpu.make_async_copy(result.at[me], mine, own_sems.at[1])
    own_block.start()

    wait_for(slab.at[pl.ds(0, n_member - 1)], send_sems.at[0])
    wait_for(part.at[pl.ds(0, n_member - 1)], send_sems.at[1])
    wait_for(rows_in.at[pl.ds(0, n_state - 1)], send_sems.at[2])
    wait_for(dist.at[pl.ds(0, n_member - 1)], send_sems.at[3])
    own_block.wait()
    wait_for(result.at[pl.ds(0, n_member - 1)], send_sems.at[4])
    wait_for(out_ref.at[:, pl.ds(0, (n_member - 1) * cols)], recv_sems.at[4])


def per_device(n_member, n_state, ensemble, obs_count):
    rows, width = ensemble.shape
    members, cols = rows * n_member, width // n_member
    half = members // 2
    return pl.pallas_call(
        functools.partial(kernel, n_member, n_state, width * n_state),
        out_shape=jax.ShapeDtypeStruct((rows, width), jnp.bfloat16),
        in_specs=[pl.BlockSpec(memory_space=pl.ANY), pl.BlockSpec(memory_space=pl.ANY)],
        out_specs=pl.BlockSpec(memory_space=pl.ANY),
        scratch_shapes=[
            pltpu.VMEM((n_member, rows, cols), jnp.bfloat16),
            pltpu.VMEM((1, members), jnp.int32),
            pltpu.VMEM((n_member, rows, half), jnp.float32),
            pltpu.VMEM((n_member, rows, half), jnp.float32),
            pltpu.VMEM((n_state, rows, half), jnp.float32),
            pltpu.VMEM((n_member, rows, half), jnp.float32),
            pltpu.VMEM((members, members), jnp.float32),
            pltpu.VMEM((n_member, rows, cols), jnp.bfloat16),
            pltpu.SemaphoreType.DMA((2,)),
            pltpu.SemaphoreType.DMA((5,)),
            pltpu.SemaphoreType.DMA((5,)),
        ],
        compiler_params=pltpu.CompilerParams(
            collective_id=0, has_side_effects=True, vmem_limit_bytes=60 * 1024 * 1024
        ),
    )(ensemble, obs_count.reshape(1, members))


def solution(mesh):
    body = functools.partial(per_device, mesh.shape["member"], mesh.shape["state"])
    return jax.shard_map(
        body, mesh=mesh, in_specs=(P("member", "state"), P()), out_specs=P("member", "state"),
        check_vma=False,
    )
```

time: 48.7 us -> 45.6 us (0.936)
  Pallas kernels: 46 us -> 43.6 us
  local copies, waits for them, and re-layouts: 2.52 us -> 1.87 us
    pallas_call x1, Pallas kernels: 46 us -> 43.6 us  [per_device(): pl.pallas_call(functools.partial(kernel, n_member, n_state, width * n_sta...]
    unnamed x5 -> x1, local copies, waits for them, and re-layouts: 2.52 us -> 1.87 us
where the time goes in v2:
time: 45.6 us; the launch traced here: 45.4 us
  Pallas kernels  43.6 us (96%)
  local copies, waits for them, and re-layouts  1.87 us (4%)
    pallas_call x1, Pallas kernels, per_device(): pl.pallas_call(functools.partial(kernel, n_member, n_state, width * n_sta...  43.6 us
    unnamed x1, local copies, waits for them, and re-layouts  1.87 us

profile of v2, /device:TPU:1, one launch (start us, length us, event | category | flops | bytes accessed | tf_op | source)
XLA Modules:
  0.0 45.4 jit_solution(12440626729466007663)
XLA Ops:
  0.0 43.6 %shard_map.28 = bf16[8,32768]{1,0:T(8,128)(2,1)} custom-call(bf16[8,32768]{1,0:T(8,128)(2,1)} %ens_ref.1, s32[1,256]{1,0:T(1,128)} %bitcast.1), custom_call_target="tpu_custom_call" | custom-call | tf_op jit(solution)/shard_map/pallas_call | solution.py:169
  43.6 1.9 %copy.4 = bf16[8,32768]{1,0:T(8,128)(2,1)} copy(bf16[8,32768]{1,0:T(8,128)(2,1)} %shard_map.28) | data formatting | bytes 1048576

commit v3 on v2

--- a/solution.py
+++ b/solution.py
@@ -14,29 +14,36 @@
 
 
 def hops(offset):
-    return sum(min(step, 4 - step) for step in offset[:2])
+    return sum(min(step, 4 - step) for step in offset[:3])
 
 
 OFFSETS = sorted(
-    ((z, y, c) for z in range(4) for y in range(4) for c in range(2) if (z, y, c) != (0, 0, 0)),
+    (
+        (x, z, y, c)
+        for x in range(4) for z in range(4) for y in range(4) for c in range(2)
+        if (x, z, y, c) != (0, 0, 0, 0)
+    ),
     key=lambda offset: -hops(offset),
 )
 
 
-def member_peers():
-    me = lax.axis_index("member")
+def others():
+    plane, me = lax.axis_index("state"), lax.axis_index("member")
     z, y, c = lax.div(me, 8), lax.rem(lax.div(me, 2), 4), lax.rem(me, 2)
-    return [
-        lax.rem(z + dz, 4) * 8 + lax.rem(y + dy, 4) * 2 + lax.rem(c + dc, 2)
-        for dz, dy, dc in OFFSETS
-    ]
+    everyone, members = [], []
+    for dx, dz, dy, dc in OFFSETS:
+        member = lax.rem(z + dz, 4) * 8 + lax.rem(y + dy, 4) * 2 + lax.rem(c + dc, 2)
+        everyone.append((lax.rem(plane + dx, 4), member))
+        if dx == 0:
+            members.append(member)
+    return everyone, members
 
 
 def kernel(
     n_member, n_state, total,
     ens_ref, obs_ref, out_ref,
-    slab, obs, part, part_in, rows_in, dist, cost_ref, result,
-    own_sems, send_sems, recv_sems,
+    slab, obs, part, part_in, dist, cost_ref, result,
+    own_sems, send_sems, recv_sems, ready_sem,
 ):
     rows = ens_ref.shape[0]
     cols = ens_ref.shape[1] // n_member
@@ -44,7 +51,9 @@
     half = members // 2
     me = lax.axis_index("member")
     plane = lax.axis_index("state")
-    peers = member_peers()
+    everyone, peers = others()
+    n_all = n_member * n_state
+    rank = plane * n_member + me
     planes = [lax.rem(plane + step, n_state) for step in range(1, n_state)]
 
     barrier = pltpu.get_barrier_semaphore()
@@ -61,6 +70,8 @@
     own_block = pltpu.make_async_copy(column_block(ens_ref, me), slab.at[me], own_sems.at[1])
     own_block.start()
     pl.semaphore_wait(barrier, n_member - 1 + n_state - 1)
+    for other in planes:
+        pl.semaphore_signal(ready_sem, inc=1, device_id={"state": other}, device_id_type=MESH)
 
     def send(source, target, phase, device):
         pltpu.make_async_remote_copy(
@@ -98,25 +109,25 @@
     norm_row = jnp.sum(diagonal, axis=0, keepdims=True)
     apart = norm_col + norm_row - 2.0 * gram
     folded = jnp.where(above, apart[:half, :half], apart[half:, half:])
-    part[: n_member // 2] = folded.reshape(n_member // 2, rows, half)
-    part[n_member // 2 :] = apart[:half, half:].reshape(n_member // 2, rows, half)
-
-    for peer in peers:
-        send(part.at[peer], part_in.at[me], 1, {"member": peer})
-    part_in[me] = part[me]
-    wait_for(part.at[pl.ds(0, n_member - 1)], recv_sems.at[1])
-    rows_in[plane] = jnp.sum(part_in[...], axis=0)
-    for other in planes:
-        send(rows_in.at[plane], rows_in.at[plane], 2, {"state": other})
-    wait_for(rows_in.at[pl.ds(0, n_state - 1)], recv_sems.at[2])
-    dist[me] = jnp.sum(rows_in[...], axis=0)
-    for peer in peers:
-        send(dist.at[me], dist.at[me], 3, {"member": peer})
-    wait_for(dist.at[pl.ds(0, n_member - 1)], recv_sems.at[3])
+    part[: n_all // 2] = folded.reshape(n_all // 2, 2, half)
+    part[n_all // 2 :] = apart[:half, half:].reshape(n_all // 2, 2, half)
+
+    pl.semaphore_wait(ready_sem, n_state - 1)
+    for other, peer in everyone:
+        send(
+            part.at[other * n_member + peer], part_in.at[rank], 1,
+            {"state": other, "member": peer},
+        )
+    part_in[rank] = part[rank]
+    wait_for(part.at[pl.ds(0, n_all - 1)], recv_sems.at[1])
+    dist[rank] = jnp.sum(part_in[...], axis=0)
+    for other, peer in everyone:
+        send(dist.at[rank], dist.at[rank], 2, {"state": other, "member": peer})
+    wait_for(dist.at[pl.ds(0, n_all - 1)], recv_sems.at[2])
 
     scale_cost = 16.0 / total * LOG2E
-    folded = dist[: n_member // 2].reshape(half, half) * scale_cost
-    across = dist[n_member // 2 :].reshape(half, half) * scale_cost
+    folded = dist[: n_all // 2].reshape(half, half) * scale_cost
+    across = dist[n_all // 2 :].reshape(half, half) * scale_cost
     first = jnp.where(above, folded, 0.0)
     second = folded - first
     cost_ref[:half, :half] = first + first.T
@@ -149,23 +160,22 @@
 
     mine = column_block(out_ref, me)
     for peer in peers:
-        send(result.at[peer], mine, 4, {"member": peer})
+        send(result.at[peer], mine, 3, {"member": peer})
     own_block = pltpu.make_async_copy(result.at[me], mine, own_sems.at[1])
     own_block.start()
 
     wait_for(slab.at[pl.ds(0, n_member - 1)], send_sems.at[0])
-    wait_for(part.at[pl.ds(0, n_member - 1)], send_sems.at[1])
-    wait_for(rows_in.at[pl.ds(0, n_state - 1)], send_sems.at[2])
-    wait_for(dist.at[pl.ds(0, n_member - 1)], send_sems.at[3])
+    wait_for(part.at[pl.ds(0, n_all - 1)], send_sems.at[1])
+    wait_for(dist.at[pl.ds(0, n_all - 1)], send_sems.at[2])
     own_block.wait()
-    wait_for(result.at[pl.ds(0, n_member - 1)], send_sems.at[4])
-    wait_for(out_ref.at[:, pl.ds(0, (n_member - 1) * cols)], recv_sems.at[4])
+    wait_for(result.at[pl.ds(0, n_member - 1)], send_sems.at[3])
+    wait_for(out_ref.at[:, pl.ds(0, (n_member - 1) * cols)], recv_sems.at[3])
 
 
 def per_device(n_member, n_state, ensemble, obs_count):
     rows, width = ensemble.shape
     members, cols = rows * n_member, width // n_member
-    half = members // 2
+    half, n_all = members // 2, n_member * n_state
     return pl.pallas_call(
         functools.partial(kernel, n_member, n_state, width * n_state),
         out_shape=jax.ShapeDtypeStruct((rows, width), jnp.bfloat16),
@@ -174,18 +184,18 @@
         scratch_shapes=[
             pltpu.VMEM((n_member, rows, cols), jnp.bfloat16),
             pltpu.VMEM((1, members), jnp.int32),
-            pltpu.VMEM((n_member, rows, half), jnp.float32),
-            pltpu.VMEM((n_member, rows, half), jnp.float32),
-            pltpu.VMEM((n_state, rows, half), jnp.float32),
-            pltpu.VMEM((n_member, rows, half), jnp.float32),
+            pltpu.VMEM((n_all, 2, half), jnp.float32),
+            pltpu.VMEM((n_all, 2, half), jnp.float32),
+            pltpu.VMEM((n_all, 2, half), jnp.float32),
             pltpu.VMEM((members, members), jnp.float32),
             pltpu.VMEM((n_member, rows, cols), jnp.bfloat16),
             pltpu.SemaphoreType.DMA((2,)),
-            pltpu.SemaphoreType.DMA((5,)),
-            pltpu.SemaphoreType.DMA((5,)),
+            pltpu.SemaphoreType.DMA((4,)),
+            pltpu.SemaphoreType.DMA((4,)),
+            pltpu.SemaphoreType.REGULAR,
         ],
         compiler_params=pltpu.CompilerParams(
-            collective_id=0, has_side_effects=True, vmem_limit_bytes=60 * 1024 * 1024
+            collective_id=0, has_side_effects=True, vmem_limit_bytes=53 * 1024 * 1024
         ),
     )(ensemble, obs_count.reshape(1, members))
 

time: 45.6 us -> 43.6 us (0.956)
  Pallas kernels: 43.6 us -> 42 us
    pallas_call x1, Pallas kernels: 43.6 us -> 42 us  [per_device(): pl.pallas_call(functools.partial(kernel, n_member, n_state, width * n_sta...]
    unnamed x1 -> x3, local copies, waits for them, and re-layouts: 1.87 us -> 1.47 us
where the time goes in v3:
time: 43.6 us; the launch traced here: 43.5 us
  Pallas kernels  42 us (96%)
  local copies, waits for them, and re-layouts  1.47 us (3%)
    pallas_call x1, Pallas kernels, per_device(): pl.pallas_call(functools.partial(kernel, n_member, n_state, width * n_sta...  42 us
    unnamed x3, local copies, waits for them, and re-layouts  1.47 us

profile of v3, /device:TPU:1, one launch (start us, length us, event | category | flops | bytes accessed | tf_op | source)
XLA Modules:
  0.0 43.5 jit_solution(10384975077692211861)
XLA Ops:
  0.0 0.0 copy-start
  0.0 0.7 %copy-done = s32[256]{0:T(256)S(1)} copy-done((s32[256]{0:T(256)S(1)}, s32[256]{0:T(256)}, u32[]{:S(2)}) %copy-start) | copy-done | bytes 1048
  0.7 42.0 %shard_map.28 = bf16[8,32768]{1,0:T(8,128)(2,1)S(1)} custom-call(bf16[8,32768]{1,0:T(8,128)(2,1)} %ens_ref.1, s32[1,256]{1,0:T(1,128)S(1)} %bitcast.1), custom_call_target="tpu_custom_call" | custom-call | tf_op jit(solution)/shard_map/pallas_call | solution.py:179
  42.7 0.8 %copy.4 = bf16[8,32768]{1,0:T(8,128)(2,1)} copy(bf16[8,32768]{1,0:T(8,128)(2,1)S(1)} %shard_map.28) | data formatting | bytes 1048576
Async XLA Ops:
  0.0 0.7 %copy-start = (s32[256]{0:T(256)S(1)}, s32[256]{0:T(256)}, u32[]{:S(2)}) copy-start(s32[256]{0:T(256)} %param.3) | copy-start | bytes 3076

commit v4 on v3

--- a/solution.py
+++ b/solution.py
@@ -136,12 +136,14 @@
     cost_ref[half:, :half] = across.T
     log_count = math.log2(members)
 
+    weight = jnp.exp2(logw)
+
     def sweep(index, carry):
         f_pot, g_pot = carry
-        cost = cost_ref[...]
-        sums = jnp.sum(jnp.exp2(g_pot + f_pot - cost), axis=0, keepdims=True)
+        scaled = jnp.exp2(g_pot + f_pot - cost_ref[...])
+        sums = jnp.sum(scaled, axis=0, keepdims=True)
         f_pot = f_pot + logw - jnp.log2(sums)
-        sums = jnp.sum(jnp.exp2(g_pot + f_pot - cost), axis=1, keepdims=True)
+        sums = jnp.sum(scaled * (weight / sums), axis=1, keepdims=True)
         g_pot = g_pot - log_count - jnp.log2(sums)
         return (f_pot, g_pot)
 
@@ -150,6 +152,7 @@
         SWEEPS,
         sweep,
         (jnp.zeros((1, members), jnp.float32), jnp.zeros((members, 1), jnp.float32)),
+        unroll=4,
     )
     plan = jnp.exp2(g_pot + f_pot - cost_ref[...] + log_count).astype(jnp.bfloat16)
     analysis = lax.dot_general(
@@ -197,7 +200,10 @@
         compiler_params=pltpu.CompilerParams(
             collective_id=0, has_side_effects=True, vmem_limit_bytes=53 * 1024 * 1024
         ),
-    )(ensemble, obs_count.reshape(1, members))
+    )(
+        pltpu.with_memory_space_constraint(ensemble, pltpu.HBM),
+        pltpu.with_memory_space_constraint(obs_count.reshape(1, members), pltpu.HBM),
+    )
 
 
 def solution(mesh):

time: 43.6 us -> 42.6 us (0.977)
  local copies, waits for them, and re-layouts: 1.47 us -> 0.8 us
    unnamed x3 -> x1, local copies, waits for them, and re-layouts: 1.47 us -> 0.8 us
where the time goes in v4:
time: 42.6 us; the launch traced here: 42.5 us
  Pallas kernels  41.7 us (98%)
  local copies, waits for them, and re-layouts  0.8 us (2%)
    pallas_call x1, Pallas kernels, per_device(): pl.pallas_call(functools.partial(kernel, n_member, n_state, width * n_sta...  41.7 us

profile of v4, /device:TPU:1, one launch (start us, length us, event | category | flops | bytes accessed | tf_op | source)
XLA Modules:
  0.0 42.5 jit_solution(17920867519437897223)
XLA Ops:
  0.0 41.7 %shard_map.28 = bf16[8,32768]{1,0:T(8,128)(2,1)S(1)} custom-call(bf16[8,32768]{1,0:T(8,128)(2,1)} %ens_ref.1, s32[1,256]{1,0:T(1,128)} %bitcast.1), custom_call_target="tpu_custom_call" | custom-call | tf_op jit(solution)/shard_map/pallas_call | solution.py:182
  41.7 0.8 %copy.4 = bf16[8,32768]{1,0:T(8,128)(2,1)} copy(bf16[8,32768]{1,0:T(8,128)(2,1)S(1)} %shard_map.28) | data formatting | bytes 1048576

commit v5 on v4

--- a/solution.py
+++ b/solution.py
@@ -25,6 +25,27 @@
     ),
     key=lambda offset: -hops(offset),
 )
+
+
+NEAR = (
+    ((2, 0), (1, 1), (1, 3), (1, 0), (3, 0), (0, 1), (0, 3), (0, 0)),
+    ((0, 2), (3, 3), (3, 1), (1, 0), (3, 0), (0, 1), (0, 3), (0, 0)),
+)
+FAR_CHIPS = 3
+
+
+def near_chips():
+    me = lax.axis_index("member")
+    z, y, c = lax.div(me, 8), lax.rem(lax.div(me, 2), 4), lax.rem(me, 2)
+    return [
+        lax.rem(z + a[0] + c * (b[0] - a[0]) + 4, 4) * 4 + lax.rem(y + a[1] + c * (b[1] - a[1]) + 4, 4)
+        for a, b in zip(*NEAR)
+    ]
+
+
+def antipode(member):
+    z, y, c = lax.div(member, 8), lax.rem(lax.div(member, 2), 4), lax.rem(member, 2)
+    return lax.rem(z + 2, 4) * 8 + lax.rem(y + 2, 4) * 2 + c
 
 
 def others():
@@ -42,7 +63,7 @@
 def kernel(
     n_member, n_state, total,
     ens_ref, obs_ref, out_ref,
-    slab, obs, part, part_in, dist, cost_ref, result,
+    slab, twin, obs, part, part_in, dist, cost_ref, plan_ref, result,
     own_sems, send_sems, recv_sems, ready_sem,
 ):
     rows = ens_ref.shape[0]
@@ -67,8 +88,11 @@
 
     own_obs = pltpu.make_async_copy(obs_ref, obs, own_sems.at[0])
     own_obs.start()
+    far = antipode(me)
     own_block = pltpu.make_async_copy(column_block(ens_ref, me), slab.at[me], own_sems.at[1])
     own_block.start()
+    own_twin = pltpu.make_async_copy(column_block(ens_ref, far), twin.at[me], own_sems.at[2])
+    own_twin.start()
     pl.semaphore_wait(barrier, n_member - 1 + n_state - 1)
     for other in planes:
         pl.semaphore_signal(ready_sem, inc=1, device_id={"state": other}, device_id_type=MESH)
@@ -118,11 +142,14 @@
             part.at[other * n_member + peer], part_in.at[rank], 1,
             {"state": other, "member": peer},
         )
+    for peer in peers[::-1]:
+        send(column_block(ens_ref, antipode(peer)), twin.at[me], 4, {"member": peer})
     part_in[rank] = part[rank]
     wait_for(part.at[pl.ds(0, n_all - 1)], recv_sems.at[1])
     dist[rank] = jnp.sum(part_in[...], axis=0)
     for other, peer in everyone:
         send(dist.at[rank], dist.at[rank], 2, {"state": other, "member": peer})
+
     wait_for(dist.at[pl.ds(0, n_all - 1)], recv_sems.at[2])
 
     scale_cost = 16.0 / total * LOG2E
@@ -155,24 +182,51 @@
         unroll=4,
     )
     plan = jnp.exp2(g_pot + f_pot - cost_ref[...] + log_count).astype(jnp.bfloat16)
-    analysis = lax.dot_general(
-        plan, slab[...].reshape(members, cols), (((1,), (0,)), ((), ())),
-        preferred_element_type=jnp.float32,
-    )
-    result[...] = analysis.reshape(n_member, rows, cols).astype(jnp.bfloat16)
-
-    mine = column_block(out_ref, me)
-    for peer in peers:
-        send(result.at[peer], mine, 3, {"member": peer})
-    own_block = pltpu.make_async_copy(result.at[me], mine, own_sems.at[1])
-    own_block.start()
+    n_chips = n_member // 2
+    plan_ref[...] = plan.reshape(n_chips, 2 * rows, members)
+    own_twin.wait()
+    wait_for(twin.at[pl.ds(0, n_member - 1)], recv_sems.at[4])
+
+    chips = near_chips()
+    served = len(chips)
+    core = lax.rem(me, 2)
+    own_sets = []
+    for start, stop in ((0, FAR_CHIPS), (FAR_CHIPS, served)):
+        mine = jnp.concatenate([plan_ref[chip] for chip in chips[start:stop]], axis=0)
+        for which, (columns, owner) in enumerate(((slab, me), (twin, far))):
+            analysis = lax.dot_general(
+                mine, columns[...].reshape(members, cols), (((1,), (0,)), ((), ())),
+                preferred_element_type=jnp.float32,
+            )
+            result[which, 2 * start : 2 * stop] = analysis.reshape(
+                2 * (stop - start), rows, cols
+            ).astype(jnp.bfloat16)
+            target = column_block(out_ref, owner)
+            for place in range(start, stop):
+                if place < served - 1:
+                    for side in range(2):
+                        send(
+                            result.at[which, 2 * place + side], target, 3,
+                            {"member": chips[place] * 2 + side},
+                        )
+                else:
+                    send(
+                        result.at[which, 2 * place + 1 - core], target, 3, {"member": me + 1 - 2 * core}
+                    )
+                    copy = pltpu.make_async_copy(
+                        result.at[which, 2 * place + core], target, own_sems.at[1 + which]
+                    )
+                    copy.start()
+                    own_sets.append(copy)
 
     wait_for(slab.at[pl.ds(0, n_member - 1)], send_sems.at[0])
     wait_for(part.at[pl.ds(0, n_all - 1)], send_sems.at[1])
     wait_for(dist.at[pl.ds(0, n_all - 1)], send_sems.at[2])
-    own_block.wait()
-    wait_for(result.at[pl.ds(0, n_member - 1)], send_sems.at[3])
-    wait_for(out_ref.at[:, pl.ds(0, (n_member - 1) * cols)], recv_sems.at[3])
+    wait_for(twin.at[pl.ds(0, n_member - 1)], send_sems.at[4])
+    for copy in own_sets:
+        copy.wait()
+    wait_for(out_ref.at[:, pl.ds(0, (n_member - 2) * cols)], send_sems.at[3])
+    wait_for(out_ref.at[:, pl.ds(0, (n_member - 2) * cols)], recv_sems.at[3])
 
 
 def per_device(n_member, n_state, ensemble, obs_count):
@@ -186,15 +240,17 @@
         out_specs=pl.BlockSpec(memory_space=pl.ANY),
         scratch_shapes=[
             pltpu.VMEM((n_member, rows, cols), jnp.bfloat16),
+            pltpu.VMEM((n_member, rows, cols), jnp.bfloat16),
             pltpu.VMEM((1, members), jnp.int32),
             pltpu.VMEM((n_all, 2, half), jnp.float32),
             pltpu.VMEM((n_all, 2, half), jnp.float32),
             pltpu.VMEM((n_all, 2, half), jnp.float32),
             pltpu.VMEM((members, members), jnp.float32),
-            pltpu.VMEM((n_member, rows, cols), jnp.bfloat16),
-            pltpu.SemaphoreType.DMA((2,)),
-            pltpu.SemaphoreType.DMA((4,)),
-            pltpu.SemaphoreType.DMA((4,)),
+            pltpu.VMEM((n_member // 2, 2 * rows, members), jnp.bfloat16),
+            pltpu.VMEM((2, n_member // 2, rows, cols), jnp.bfloat16),
+            pltpu.SemaphoreType.DMA((3,)),
+            pltpu.SemaphoreType.DMA((5,)),
+            pltpu.SemaphoreType.DMA((5,)),
             pltpu.SemaphoreType.REGULAR,
         ],
         compiler_params=pltpu.CompilerParams(

time: 42.6 us -> 41 us (0.962)
  Pallas kernels: 41.7 us -> 40.1 us
    pallas_call x1, Pallas kernels: 41.7 us -> 40.1 us  [per_device(): pl.pallas_call(functools.partial(kernel, n_member, n_state, width * n_sta...]
where the time goes in v5:
time: 41 us; the launch traced here: 40.9 us
  Pallas kernels  40.1 us (98%)
  local copies, waits for them, and re-layouts  0.8 us (2%)
    pallas_call x1, Pallas kernels, per_device(): pl.pallas_call(functools.partial(kernel, n_member, n_state, width * n_sta...  40.1 us

profile of v5, /device:TPU:1, one launch (start us, length us, event | category | flops | bytes accessed | tf_op | source)
XLA Modules:
  0.0 40.9 jit_solution(18244727116729551376)
XLA Ops:
  0.0 40.1 %shard_map.28 = bf16[8,32768]{1,0:T(8,128)(2,1)S(1)} custom-call(bf16[8,32768]{1,0:T(8,128)(2,1)} %ens_ref.1, s32[1,256]{1,0:T(1,128)} %bitcast.1), custom_call_target="tpu_custom_call" | custom-call | tf_op jit(solution)/shard_map/pallas_call | solution.py:236
  40.1 0.8 %copy.4 = bf16[8,32768]{1,0:T(8,128)(2,1)} copy(bf16[8,32768]{1,0:T(8,128)(2,1)S(1)} %shard_map.28) | data formatting | bytes 1048576

commit v6 on v5

--- a/solution.py
+++ b/solution.py
@@ -13,8 +13,9 @@
 LOG2E = math.log2(math.e)
 
 
-def hops(offset):
-    return sum(min(step, 4 - step) for step in offset[:3])
+def nearness(offset):
+    steps = [min(step, 4 - step) for step in offset[:3]]
+    return (-sum(steps), max(steps), offset[3])
 
 
 OFFSETS = sorted(
@@ -23,7 +24,7 @@
         for x in range(4) for z in range(4) for y in range(4) for c in range(2)
         if (x, z, y, c) != (0, 0, 0, 0)
     ),
-    key=lambda offset: -hops(offset),
+    key=nearness,
 )
 
 
@@ -51,19 +52,23 @@
 def others():
     plane, me = lax.axis_index("state"), lax.axis_index("member")
     z, y, c = lax.div(me, 8), lax.rem(lax.div(me, 2), 4), lax.rem(me, 2)
-    everyone, members = [], []
-    for dx, dz, dy, dc in OFFSETS:
-        member = lax.rem(z + dz, 4) * 8 + lax.rem(y + dy, 4) * 2 + lax.rem(c + dc, 2)
-        everyone.append((lax.rem(plane + dx, 4), member))
-        if dx == 0:
-            members.append(member)
-    return everyone, members
+    planes = [lax.rem(plane + step, 4) for step in range(4)]
+    layers = [lax.rem(z + step, 4) * 8 for step in range(4)]
+    lines = [lax.rem(y + step, 4) * 2 for step in range(4)]
+    cores = [c, 1 - c]
+    members = {
+        (dz, dy, dc): layers[dz] + lines[dy] + cores[dc]
+        for dz in range(4) for dy in range(4) for dc in range(2)
+    }
+    everyone = [(planes[dx], members[dz, dy, dc]) for dx, dz, dy, dc in OFFSETS]
+    peers = [members[dz, dy, dc] for dx, dz, dy, dc in OFFSETS if dx == 0]
+    return everyone, peers
 
 
 def kernel(
     n_member, n_state, total,
     ens_ref, obs_ref, out_ref,
-    slab, twin, obs, part, part_in, dist, cost_ref, plan_ref, result,
+    own, slab, twin, obs, part, part_in, dist, cost_ref, plan_ref, result,
     own_sems, send_sems, recv_sems, ready_sem,
 ):
     rows = ens_ref.shape[0]
@@ -88,6 +93,8 @@
 
     own_obs = pltpu.make_async_copy(obs_ref, obs, own_sems.at[0])
     own_obs.start()
+    staged = pltpu.make_async_copy(ens_ref, own, own_sems.at[3])
+    staged.start()
     far = antipode(me)
     own_block = pltpu.make_async_copy(column_block(ens_ref, me), slab.at[me], own_sems.at[1])
     own_block.start()
@@ -110,8 +117,9 @@
     def wait_for(ref, sem):
         pltpu.make_async_copy(ref, ref, sem).wait()
 
+    staged.wait()
     for peer in peers:
-        send(column_block(ens_ref, peer), slab.at[me], 0, {"member": peer})
+        send(column_block(own, peer), slab.at[me], 0, {"member": peer})
 
     own_obs.wait()
     raw = -2.0 * obs[...].astype(jnp.float32)
@@ -142,14 +150,17 @@
             part.at[other * n_member + peer], part_in.at[rank], 1,
             {"state": other, "member": peer},
         )
-    for peer in peers[::-1]:
-        send(column_block(ens_ref, antipode(peer)), twin.at[me], 4, {"member": peer})
+    for peer in peers[:8:-1]:
+        send(column_block(own, antipode(peer)), twin.at[me], 4, {"member": peer})
     part_in[rank] = part[rank]
     wait_for(part.at[pl.ds(0, n_all - 1)], recv_sems.at[1])
-    dist[rank] = jnp.sum(part_in[...], axis=0)
+    sums = jnp.sum(part_in[...].reshape(members // 8, 8, half), axis=0)
+    dist[rank] = sums[0:2] + sums[2:4] + (sums[4:6] + sums[6:8])
     for other, peer in everyone:
         send(dist.at[rank], dist.at[rank], 2, {"state": other, "member": peer})
 
+    for peer in peers[8::-1]:
+        send(column_block(own, antipode(peer)), twin.at[me], 4, {"member": peer})
     wait_for(dist.at[pl.ds(0, n_all - 1)], recv_sems.at[2])
 
     scale_cost = 16.0 / total * LOG2E
@@ -191,33 +202,22 @@
     served = len(chips)
     core = lax.rem(me, 2)
     own_sets = []
-    for start, stop in ((0, FAR_CHIPS), (FAR_CHIPS, served)):
-        mine = jnp.concatenate([plan_ref[chip] for chip in chips[start:stop]], axis=0)
-        for which, (columns, owner) in enumerate(((slab, me), (twin, far))):
-            analysis = lax.dot_general(
-                mine, columns[...].reshape(members, cols), (((1,), (0,)), ((), ())),
-                preferred_element_type=jnp.float32,
-            )
-            result[which, 2 * start : 2 * stop] = analysis.reshape(
-                2 * (stop - start), rows, cols
-            ).astype(jnp.bfloat16)
-            target = column_block(out_ref, owner)
-            for place in range(start, stop):
-                if place < served - 1:
-                    for side in range(2):
-                        send(
-                            result.at[which, 2 * place + side], target, 3,
-                            {"member": chips[place] * 2 + side},
-                        )
-                else:
-                    send(
-                        result.at[which, 2 * place + 1 - core], target, 3, {"member": me + 1 - 2 * core}
-                    )
-                    copy = pltpu.make_async_copy(
-                        result.at[which, 2 * place + core], target, own_sems.at[1 + which]
-                    )
-                    copy.start()
-                    own_sets.append(copy)
+    mine = jnp.concatenate([plan_ref[chip] for chip in chips], axis=0)
+    for which, (columns, owner) in enumerate(((slab, me), (twin, far))):
+        analysis = lax.dot_general(
+            mine, columns[...].reshape(members, cols), (((1,), (0,)), ((), ())),
+            preferred_element_type=jnp.float32,
+        )
+        result[which] = analysis.reshape(2 * served, rows, cols).astype(jnp.bfloat16)
+        target = column_block(out_ref, owner)
+        for place, chip in enumerate(chips[:-1]):
+            for side in range(2):
+                send(result.at[which, 2 * place + side], target, 3, {"member": chip * 2 + side})
+        last = 2 * (served - 1)
+        send(result.at[which, last + 1 - core], target, 3, {"member": me + 1 - 2 * core})
+        copy = pltpu.make_async_copy(result.at[which, last + core], target, own_sems.at[1 + which])
+        copy.start()
+        own_sets.append(copy)
 
     wait_for(slab.at[pl.ds(0, n_member - 1)], send_sems.at[0])
     wait_for(part.at[pl.ds(0, n_all - 1)], send_sems.at[1])
@@ -239,6 +239,7 @@
         in_specs=[pl.BlockSpec(memory_space=pl.ANY), pl.BlockSpec(memory_space=pl.ANY)],
         out_specs=pl.BlockSpec(memory_space=pl.ANY),
         scratch_shapes=[
+            pltpu.VMEM((rows, width), jnp.bfloat16),
             pltpu.VMEM((n_member, rows, cols), jnp.bfloat16),
             pltpu.VMEM((n_member, rows, cols), jnp.bfloat16),
             pltpu.VMEM((1, members), jnp.int32),
@@ -248,7 +249,7 @@
             pltpu.VMEM((members, members), jnp.float32),
             pltpu.VMEM((n_member // 2, 2 * rows, members), jnp.bfloat16),
             pltpu.VMEM((2, n_member // 2, rows, cols), jnp.bfloat16),
-            pltpu.SemaphoreType.DMA((3,)),
+            pltpu.SemaphoreType.DMA((4,)),
             pltpu.SemaphoreType.DMA((5,)),
             pltpu.SemaphoreType.DMA((5,)),
             pltpu.SemaphoreType.REGULAR,

time: 41 us -> 40.1 us (0.978)
  Pallas kernels: 40.1 us -> 39.2 us
    pallas_call x1, Pallas kernels: 40.1 us -> 39.2 us  [per_device(): pl.pallas_call(functools.partial(kernel, n_member, n_state, width * n_sta...]
where the time goes in v6:
time: 40.1 us; the launch traced here: 40 us
  Pallas kernels  39.2 us (98%)
  local copies, waits for them, and re-layouts  0.8 us (2%)
    pallas_call x1, Pallas kernels, per_device(): pl.pallas_call(functools.partial(kernel, n_member, n_state, width * n_sta...  39.2 us

profile of v6, /device:TPU:1, one launch (start us, length us, event | category | flops | bytes accessed | tf_op | source)
XLA Modules:
  0.0 40.0 jit_solution(15653634234842294571)
XLA Ops:
  0.0 39.2 %shard_map.28 = bf16[8,32768]{1,0:T(8,128)(2,1)S(1)} custom-call(bf16[8,32768]{1,0:T(8,128)(2,1)} %ens_ref.1, s32[1,256]{1,0:T(1,128)} %bitcast.1), custom_call_target="tpu_custom_call" | custom-call | tf_op jit(solution)/shard_map/pallas_call | solution.py:236
  39.2 0.8 %copy.4 = bf16[8,32768]{1,0:T(8,128)(2,1)} copy(bf16[8,32768]{1,0:T(8,128)(2,1)S(1)} %shard_map.28) | data formatting | bytes 1048576

commit v7 on v6

--- a/solution.py
+++ b/solution.py
@@ -156,8 +156,13 @@
     wait_for(part.at[pl.ds(0, n_all - 1)], recv_sems.at[1])
     sums = jnp.sum(part_in[...].reshape(members // 8, 8, half), axis=0)
     dist[rank] = sums[0:2] + sums[2:4] + (sums[4:6] + sums[6:8])
-    for other, peer in everyone:
-        send(dist.at[rank], dist.at[rank], 2, {"state": other, "member": peer})
+    for other in range(n_state):
+        for peer in peers:
+            send(dist.at[rank], dist.at[rank], 2, {"state": other, "member": peer})
+
+        @pl.when(plane != other)
+        def _():
+            send(dist.at[rank], dist.at[rank], 2, {"state": other, "member": me})
 
     for peer in peers[8::-1]:
         send(column_block(own, antipode(peer)), twin.at[me], 4, {"member": peer})
@@ -201,23 +206,39 @@
     chips = near_chips()
     served = len(chips)
     core = lax.rem(me, 2)
-    own_sets = []
     mine = jnp.concatenate([plan_ref[chip] for chip in chips], axis=0)
-    for which, (columns, owner) in enumerate(((slab, me), (twin, far))):
+    for which, columns in enumerate((slab, twin)):
         analysis = lax.dot_general(
             mine, columns[...].reshape(members, cols), (((1,), (0,)), ((), ())),
             preferred_element_type=jnp.float32,
         )
         result[which] = analysis.reshape(2 * served, rows, cols).astype(jnp.bfloat16)
-        target = column_block(out_ref, owner)
-        for place, chip in enumerate(chips[:-1]):
-            for side in range(2):
-                send(result.at[which, 2 * place + side], target, 3, {"member": chip * 2 + side})
-        last = 2 * (served - 1)
-        send(result.at[which, last + 1 - core], target, 3, {"member": me + 1 - 2 * core})
-        copy = pltpu.make_async_copy(result.at[which, last + core], target, own_sems.at[1 + which])
+
+    def serve(place):
+        for which, owner in enumerate((me, far)):
+            target = column_block(out_ref, owner)
+            if place < served - 1:
+                for side in range(2):
+                    send(
+                        result.at[which, 2 * place + side], target, 3,
+                        {"member": chips[place] * 2 + side},
+                    )
+            else:
+                send(
+                    result.at[which, 2 * place + 1 - core], target, 3, {"member": me + 1 - 2 * core}
+                )
+
+    for turn in range(4):
+        for place in range(served):
+            pl.when(lax.div(chips[place], 4) == turn)(functools.partial(serve, place))
+    own_sets = [
+        pltpu.make_async_copy(
+            result.at[which, 2 * (served - 1) + core], column_block(out_ref, owner), own_sems.at[1 + which]
+        )
+        for which, owner in enumerate((me, far))
+    ]
+    for copy in own_sets:
         copy.start()
-        own_sets.append(copy)
 
     wait_for(slab.at[pl.ds(0, n_member - 1)], send_sems.at[0])
     wait_for(part.at[pl.ds(0, n_all - 1)], send_sems.at[1])

time: 40.1 us -> 39.9 us (level)
  no operation moved by 1% of the time
where the time goes in v7:
time: 39.9 us; the launch traced here: 39.8 us
  Pallas kernels  39 us (98%)
  local copies, waits for them, and re-layouts  0.8 us (2%)
    pallas_call x1, Pallas kernels, per_device(): pl.pallas_call(functools.partial(kernel, n_member, n_state, width * n_sta...  39 us

profile of v7, /device:TPU:1, one launch (start us, length us, event | category | flops | bytes accessed | tf_op | source)
XLA Modules:
  0.0 39.8 jit_solution(17301818513518023830)
XLA Ops:
  0.0 39.0 %shard_map.28 = bf16[8,32768]{1,0:T(8,128)(2,1)S(1)} custom-call(bf16[8,32768]{1,0:T(8,128)(2,1)} %ens_ref.1, s32[1,256]{1,0:T(1,128)} %bitcast.1), custom_call_target="tpu_custom_call" | custom-call | tf_op jit(solution)/shard_map/pallas_call | solution.py:257
  39.0 0.8 %copy.4 = bf16[8,32768]{1,0:T(8,128)(2,1)} copy(bf16[8,32768]{1,0:T(8,128)(2,1)S(1)} %shard_map.28) | data formatting | bytes 1048576

commit v8 on v7

--- a/solution.py
+++ b/solution.py
@@ -9,6 +9,7 @@
 from jax.sharding import PartitionSpec as P
 
 SWEEPS = 20
+LIFT = 80.0
 MESH = pl.DeviceIdType.MESH
 LOG2E = math.log2(math.e)
 
@@ -179,23 +180,27 @@
     cost_ref[half:, :half] = across.T
     log_count = math.log2(members)
 
-    weight = jnp.exp2(logw)
-
-    def sweep(index, carry):
+    weight = jnp.exp2(logw + LIFT)
+
+    def two_sweeps(index, carry):
         f_pot, g_pot = carry
-        scaled = jnp.exp2(g_pot + f_pot - cost_ref[...])
-        sums = jnp.sum(scaled, axis=0, keepdims=True)
-        f_pot = f_pot + logw - jnp.log2(sums)
-        sums = jnp.sum(scaled * (weight / sums), axis=1, keepdims=True)
-        g_pot = g_pot - log_count - jnp.log2(sums)
+        scaled = jnp.exp2(g_pot + (f_pot + LIFT) - cost_ref[...])
+        for again in (True, False):
+            sums = jnp.sum(scaled, axis=0, keepdims=True)
+            f_pot = f_pot + ((logw + LIFT) - jnp.log2(sums))
+            scaled = scaled * (weight / sums)
+            sums = jnp.sum(scaled, axis=1, keepdims=True)
+            g_pot = g_pot + ((LIFT - log_count) - jnp.log2(sums))
+            if again:
+                scaled = scaled * (2.0 ** (LIFT - log_count) / sums)
         return (f_pot, g_pot)
 
     f_pot, g_pot = lax.fori_loop(
         0,
-        SWEEPS,
-        sweep,
+        SWEEPS // 2,
+        two_sweeps,
         (jnp.zeros((1, members), jnp.float32), jnp.zeros((members, 1), jnp.float32)),
-        unroll=4,
+        unroll=5,
     )
     plan = jnp.exp2(g_pot + f_pot - cost_ref[...] + log_count).astype(jnp.bfloat16)
     n_chips = n_member // 2

time: 39.9 us -> 39.6 us (level)
  no operation moved by 1% of the time
where the time goes in v8:
time: 39.6 us; the launch traced here: 39.5 us
  Pallas kernels  38.7 us (98%)
  local copies, waits for them, and re-layouts  0.8 us (2%)
    pallas_call x1, Pallas kernels, per_device(): pl.pallas_call(functools.partial(kernel, n_member, n_state, width * n_sta...  38.7 us
    unnamed x1, local copies, waits for them, and re-layouts  0.8 us

profile of v8, /device:TPU:1, one launch (start us, length us, event | category | flops | bytes accessed | tf_op | source)
XLA Modules:
  0.0 39.5 jit_solution(17217110217348944572)
XLA Ops:
  0.0 38.7 %shard_map.28 = bf16[8,32768]{1,0:T(8,128)(2,1)S(1)} custom-call(bf16[8,32768]{1,0:T(8,128)(2,1)} %ens_ref.1, s32[1,256]{1,0:T(1,128)} %bitcast.1), custom_call_target="tpu_custom_call" | custom-call | tf_op jit(solution)/shard_map/pallas_call | solution.py:262
  38.7 0.8 %copy.4 = bf16[8,32768]{1,0:T(8,128)(2,1)} copy(bf16[8,32768]{1,0:T(8,128)(2,1)S(1)} %shard_map.28) | data formatting | bytes 1048576

commit v9 on v8

--- a/solution.py
+++ b/solution.py
@@ -197,12 +197,16 @@
 
     f_pot, g_pot = lax.fori_loop(
         0,
-        SWEEPS // 2,
+        SWEEPS // 2 - 1,
         two_sweeps,
         (jnp.zeros((1, members), jnp.float32), jnp.zeros((members, 1), jnp.float32)),
-        unroll=5,
+        unroll=3,
     )
-    plan = jnp.exp2(g_pot + f_pot - cost_ref[...] + log_count).astype(jnp.bfloat16)
+    scaled = jnp.exp2(g_pot + (f_pot + LIFT) - cost_ref[...])
+    scaled = scaled * (weight / jnp.sum(scaled, axis=0, keepdims=True))
+    scaled = scaled * (2.0 ** (LIFT - log_count) / jnp.sum(scaled, axis=1, keepdims=True))
+    scaled = scaled * (weight / jnp.sum(scaled, axis=0, keepdims=True))
+    plan = (scaled * (1.0 / jnp.sum(scaled, axis=1, keepdims=True))).astype(jnp.bfloat16)
     n_chips = n_member // 2
     plan_ref[...] = plan.reshape(n_chips, 2 * rows, members)
     own_twin.wait()

time: 39.6 us -> 39.6 us (level)
  no operation moved by 1% of the time
where the time goes in v9:
time: 39.6 us; the launch traced here: 39.5 us
  Pallas kernels  38.7 us (98%)
  local copies, waits for them, and re-layouts  0.8 us (2%)
    pallas_call x1, Pallas kernels, per_device(): pl.pallas_call(functools.partial(kernel, n_member, n_state, width * n_sta...  38.7 us
    unnamed x1, local copies, waits for them, and re-layouts  0.8 us

profile of v9, /device:TPU:1, one launch (start us, length us, event | category | flops | bytes accessed | tf_op | source)
XLA Modules:
  0.0 39.5 jit_solution(3461936885804301629)
XLA Ops:
  0.0 38.7 %shard_map.28 = bf16[8,32768]{1,0:T(8,128)(2,1)S(1)} custom-call(bf16[8,32768]{1,0:T(8,128)(2,1)} %ens_ref.1, s32[1,256]{1,0:T(1,128)} %bitcast.1), custom_call_target="tpu_custom_call" | custom-call | tf_op jit(solution)/shard_map/pallas_call | solution.py:266
  38.7 0.8 %copy.4 = bf16[8,32768]{1,0:T(8,128)(2,1)} copy(bf16[8,32768]{1,0:T(8,128)(2,1)S(1)} %shard_map.28) | data formatting | bytes 1048576

commit v10 on v9

--- a/solution.py
+++ b/solution.py
@@ -118,8 +118,10 @@
     def wait_for(ref, sem):
         pltpu.make_async_copy(ref, ref, sem).wait()
 
+    for peer in peers[:12]:
+        send(column_block(ens_ref, peer), slab.at[me], 0, {"member": peer})
     staged.wait()
-    for peer in peers:
+    for peer in peers[12:]:
         send(column_block(own, peer), slab.at[me], 0, {"member": peer})
 
     own_obs.wait()

time: 39.6 us -> 39.3 us (level)
  no operation moved by 1% of the time
where the time goes in v10:
time: 39.3 us; the launch traced here: 39.2 us
  Pallas kernels  38.4 us (98%)
  local copies, waits for them, and re-layouts  0.8 us (2%)
    pallas_call x1, Pallas kernels, per_device(): pl.pallas_call(functools.partial(kernel, n_member, n_state, width * n_sta...  38.4 us
    unnamed x1, local copies, waits for them, and re-layouts  0.8 us

profile of v10, /device:TPU:1, one launch (start us, length us, event | category | flops | bytes accessed | tf_op | source)
XLA Modules:
  0.0 39.2 jit_solution(696119775834727023)
XLA Ops:
  0.0 38.4 %shard_map.28 = bf16[8,32768]{1,0:T(8,128)(2,1)S(1)} custom-call(bf16[8,32768]{1,0:T(8,128)(2,1)} %ens_ref.1, s32[1,256]{1,0:T(1,128)} %bitcast.1), custom_call_target="tpu_custom_call" | custom-call | tf_op jit(solution)/shard_map/pallas_call | solution.py:268
  38.4 0.8 %copy.4 = bf16[8,32768]{1,0:T(8,128)(2,1)} copy(bf16[8,32768]{1,0:T(8,128)(2,1)S(1)} %shard_map.28) | data formatting | bytes 1048576

commit v11 on v10

--- a/solution.py
+++ b/solution.py
@@ -100,7 +100,6 @@
     own_block = pltpu.make_async_copy(column_block(ens_ref, me), slab.at[me], own_sems.at[1])
     own_block.start()
     own_twin = pltpu.make_async_copy(column_block(ens_ref, far), twin.at[me], own_sems.at[2])
-    own_twin.start()
     pl.semaphore_wait(barrier, n_member - 1 + n_state - 1)
     for other in planes:
         pl.semaphore_signal(ready_sem, inc=1, device_id={"state": other}, device_id_type=MESH)
@@ -118,11 +117,12 @@
     def wait_for(ref, sem):
         pltpu.make_async_copy(ref, ref, sem).wait()
 
-    for peer in peers[:12]:
+    for peer in peers[:9]:
         send(column_block(ens_ref, peer), slab.at[me], 0, {"member": peer})
     staged.wait()
-    for peer in peers[12:]:
+    for peer in peers[9:]:
         send(column_block(own, peer), slab.at[me], 0, {"member": peer})
+    own_twin.start()
 
     own_obs.wait()
     raw = -2.0 * obs[...].astype(jnp.float32)

time: 39.3 us -> 39.3 us (level)
  no operation moved by 1% of the time
where the time goes in v11:
time: 39.3 us; the launch traced here: 39.2 us
  Pallas kernels  38.4 us (98%)
  local copies, waits for them, and re-layouts  0.8 us (2%)
    pallas_call x1, Pallas kernels, per_device(): pl.pallas_call(functools.partial(kernel, n_member, n_state, width * n_sta...  38.4 us
    unnamed x1, local copies, waits for them, and re-layouts  0.8 us

profile of v11, /device:TPU:1, one launch (start us, length us, event | category | flops | bytes accessed | tf_op | source)
XLA Modules:
  0.0 39.2 jit_solution(3366936056053844866)
XLA Ops:
  0.0 38.4 %shard_map.28 = bf16[8,32768]{1,0:T(8,128)(2,1)S(1)} custom-call(bf16[8,32768]{1,0:T(8,128)(2,1)} %ens_ref.1, s32[1,256]{1,0:T(1,128)} %bitcast.1), custom_call_target="tpu_custom_call" | custom-call | tf_op jit(solution)/shard_map/pallas_call | solution.py:268
  38.4 0.8 %copy.4 = bf16[8,32768]{1,0:T(8,128)(2,1)} copy(bf16[8,32768]{1,0:T(8,128)(2,1)S(1)} %shard_map.28) | data formatting | bytes 1048576

commit v12 on v11

--- a/solution.py
+++ b/solution.py
@@ -98,7 +98,6 @@
     staged.start()
     far = antipode(me)
     own_block = pltpu.make_async_copy(column_block(ens_ref, me), slab.at[me], own_sems.at[1])
-    own_block.start()
     own_twin = pltpu.make_async_copy(column_block(ens_ref, far), twin.at[me], own_sems.at[2])
     pl.semaphore_wait(barrier, n_member - 1 + n_state - 1)
     for other in planes:
@@ -122,6 +121,7 @@
     staged.wait()
     for peer in peers[9:]:
         send(column_block(own, peer), slab.at[me], 0, {"member": peer})
+    own_block.start()
     own_twin.start()
 
     own_obs.wait()

time: 39.3 us -> 39.4 us (level)
  no operation moved by 1% of the time
where the time goes in v12:
time: 39.4 us; the launch traced here: 39.2 us
  Pallas kernels  38.4 us (97%)
  local copies, waits for them, and re-layouts  0.8 us (2%)
    pallas_call x1, Pallas kernels, per_device(): pl.pallas_call(functools.partial(kernel, n_member, n_state, width * n_sta...  38.4 us
    unnamed x1, local copies, waits for them, and re-layouts  0.8 us

profile of v12, /device:TPU:1, one launch (start us, length us, event | category | flops | bytes accessed | tf_op | source)
XLA Modules:
  0.0 39.2 jit_solution(3693084842703404291)
XLA Ops:
  0.0 38.4 %shard_map.28 = bf16[8,32768]{1,0:T(8,128)(2,1)S(1)} custom-call(bf16[8,32768]{1,0:T(8,128)(2,1)} %ens_ref.1, s32[1,256]{1,0:T(1,128)} %bitcast.1), custom_call_target="tpu_custom_call" | custom-call | tf_op jit(solution)/shard_map/pallas_call | solution.py:268
  38.4 0.8 %copy.4 = bf16[8,32768]{1,0:T(8,128)(2,1)} copy(bf16[8,32768]{1,0:T(8,128)(2,1)S(1)} %shard_map.28) | data formatting | bytes 1048576
